TPU v7x, 128 devices: a whole 4x4x4 slice. The times are simulated.
128 devices in a mesh: group: 16 (over x, z), owner: 8 (over y, core).
Axes of the slice: x: 4, y: 4, z: 4, core: 2. Of those that a mesh axis runs over, the one named last changes fastest.
Arguments:
- embeddings: bfloat16 [131072, 1024], P(('group', 'owner')), may hold values from -2 to 2
- home_pairs: int32 [16, 8, 5, 64, 2], P('group', 'owner'), may hold values from 0 to 7, as said below
- home_count: int32 [16, 8, 5], P('group', 'owner'), may hold values from 0 to 20
- surplus_pairs: int32 [16, 8, 16, 3], P('group', 'owner'), may hold values from 0 to 7, as said below
Outputs:
- centered: bfloat16 [131072, 1024], P(('group', 'owner'))
- log_density: float32 [131072], P(('group', 'owner'))
Inputs may be any that keep to these rules, and one draw needn't show every extreme that they name: `home_pairs`: for owner o of group g and distance s, the first home_count[g, o, s] slots hold distinct pairs (a, b) of block a of owner o and block b of owner (o + s) mod 8 that lie in one cluster; at distance 0 a <= b and every pair (a, a) is listed; at twice s equal to 8 only owners below 4 list pairs; later slots are ignored. `surplus_pairs`: A live entry (a, b, 1) names two blocks of the same owner in one cluster with a < b; no pair is live twice or also listed in home_pairs; dead entries are ignored.
All inputs are finite; a program needn't handle non-finite values.
Results may differ from a plain program's by a relative error of at most 0.0057.
Values may be sent and summed in bfloat16 or wider, within the bound.
No kernel may reach another device: no remote copies, remote signals or barrier semaphores. Data moves between devices by JAX's collectives and lax.ppermute only.
A program may use at most 128 MiB of HBM per device.

v0:
```python
import jax
import jax.numpy as jnp
from jax import lax
from jax.sharding import PartitionSpec as P

BLOCK = 128


sharpness = 4.0
epsilon = 1e-06


def passed_along(block, axis, distance):
    devices = range(lax.axis_size(axis))
    route = [((i - distance) % len(devices), i) for i in devices]
    return lax.ppermute(block, axis, route)


def unit_rows(embeddings):
    widened = embeddings.astype(jnp.float32)
    inv_rms = lax.rsqrt(jnp.mean(widened * widened, axis=-1, keepdims=True) + epsilon)
    return (widened * inv_rms).astype(jnp.bfloat16)


def pair_terms(first_block, second_block):
    embed_width = first_block.shape[-1]
    similarity = jnp.einsum(
        "nid,njd->nij", first_block, second_block, preferred_element_type=jnp.float32
    ) * (1.0 / embed_width)
    kernel = jnp.exp(sharpness * (similarity - 1.0))
    kernel_low = kernel.astype(jnp.bfloat16)
    to_first = jnp.einsum(
        "nij,njd->nid", kernel_low, second_block, preferred_element_type=jnp.float32
    )
    to_second = jnp.einsum(
        "nij,nid->njd", kernel_low, first_block, preferred_element_type=jnp.float32
    )
    return (to_first, to_second, jnp.sum(kernel, axis=2), jnp.sum(kernel, axis=1))


def score_slots(pair_tiles):
    leading = pair_tiles.shape[:2]
    flat_pairs = pair_tiles.reshape((leading[0] * leading[1],) + pair_tiles.shape[2:])

    def score_pair(one_pair):
        to_first, to_second, dens_first, dens_second = pair_terms(
            one_pair[0][None], one_pair[1][None]
        )
        tile_sums = jnp.concatenate([to_first, to_second], axis=0).astype(jnp.bfloat16)
        tile_dens = jnp.concatenate([dens_first, dens_second], axis=0).astype(jnp.bfloat16)
        return (tile_sums, tile_dens)

    tile_sums, tile_dens = lax.map(score_pair, flat_pairs)
    return (
        tile_sums.reshape(leading + tile_sums.shape[1:]),
        tile_dens.reshape(leading + tile_dens.shape[1:]),
    )


def make_step(blocks, partner, pair_list, number, batch_size, skip_self):

    def step(turn_index, carry):
        near_sums, near_dens, far_sums, far_dens = carry
        chosen = lax.dynamic_slice_in_dim(pair_list, turn_index * batch_size, batch_size, 0)
        positions = turn_index * batch_size + jnp.arange(batch_size, dtype=jnp.int32)
        keep_mask = (positions < number).astype(jnp.float32)
        first_ids = chosen[:, 0]
        second_ids = chosen[:, 1]
        to_first, to_second, dens_first, dens_second = pair_terms(
            blocks[first_ids], partner[second_ids]
        )
        other_mask = keep_mask
        if skip_self:
            other_mask = keep_mask * (first_ids != second_ids).astype(jnp.float32)
        near_sums = near_sums.at[first_ids].add(to_first * keep_mask[:, None, None])
        near_dens = near_dens.at[first_ids].add(dens_first * keep_mask[:, None])
        far_sums = far_sums.at[second_ids].add(to_second * other_mask[:, None, None])
        far_dens = far_dens.at[second_ids].add(dens_second * other_mask[:, None])
        return (near_sums, near_dens, far_sums, far_dens)

    return step


def shards(embeddings, home_pairs, home_count, surplus_pairs):
    normed = unit_rows(embeddings)
    embed_width = normed.shape[1]
    blocks = normed.reshape(-1, BLOCK, embed_width)
    block_count = blocks.shape[0]
    slot_count = home_pairs.shape[3]
    batch_size = min(4, slot_count)
    near_sums = jnp.zeros((block_count, BLOCK, embed_width), jnp.float32)
    near_dens = jnp.zeros((block_count, BLOCK), jnp.float32)
    for distance in range(lax.axis_size("owner") // 2 + 1):
        if distance == 0:
            partner = blocks
        else:
            partner = passed_along(blocks, "owner", -distance)
        pair_list = home_pairs[0, 0, distance]
        number = home_count[0, 0, distance]
        far_sums = jnp.zeros_like(near_sums)
        far_dens = jnp.zeros_like(near_dens)
        step = make_step(blocks, partner, pair_list, number, batch_size, distance == 0)
        turn_count = (number + batch_size - 1) // batch_size
        near_sums, near_dens, far_sums, far_dens = lax.fori_loop(
            0, turn_count, step, (near_sums, near_dens, far_sums, far_dens)
        )
        if distance == 0:
            near_sums = near_sums + far_sums
            near_dens = near_dens + far_dens
        else:
            back_sums, back_dens = passed_along(
                (far_sums.astype(jnp.bfloat16), far_dens.astype(jnp.bfloat16)), "owner", distance
            )
            near_sums = near_sums + back_sums.astype(jnp.float32)
            near_dens = near_dens + back_dens.astype(jnp.float32)
    surplus_plan = surplus_pairs[0, 0]
    first_ids = surplus_plan[:, 0]
    second_ids = surplus_plan[:, 1]
    live_mask = surplus_plan[:, 2].astype(jnp.float32)
    pair_tiles = jnp.stack([blocks[first_ids], blocks[second_ids]], axis=1)[:, None]
    tile_sums, tile_dens = score_slots(pair_tiles)
    tile_sums = tile_sums[:, 0].astype(jnp.float32) * live_mask[:, None, None, None]
    tile_dens = tile_dens[:, 0].astype(jnp.float32) * live_mask[:, None, None]
    near_sums = near_sums.at[first_ids].add(tile_sums[:, 0]).at[second_ids].add(tile_sums[:, 1])
    near_dens = near_dens.at[first_ids].add(tile_dens[:, 0]).at[second_ids].add(tile_dens[:, 1])
    log_density = jnp.log(near_dens).reshape(-1)
    centered = (blocks.astype(jnp.float32) - near_sums / near_dens[..., None]).astype(jnp.bfloat16)
    return (centered.reshape(-1, embed_width), log_density)


def solution(mesh):
    return jax.shard_map(
        shards,
        mesh=mesh,
        in_specs=(
            P(("group", "owner"), None),
            P("group", "owner", None, None, None),
            P("group", "owner", None),
            P("group", "owner", None, None),
        ),
        out_specs=(P(("group", "owner"), None), P(("group", "owner"))),
        check_vma=False,
    )
```

profile of v0, /device:TPU:102, one launch (start us, length us, event | category | flops | bytes accessed | tf_op | source)
XLA Modules:
  0.0 534.8 jit_solution(12611806479623578135)
XLA Ops:
  15.4 36.4 %while.104 = (s32[]{:T(128)}, f32[8,128,1024]{2,1,0:T(8,128)}, f32[8,128]{1,0:T(8,128)S(1)}, f32[8,128,1024]{2,1,0:T(8,128)}, f32[8,128]{1,0:T(8,128)S(1)}, /*in...) while((s32[]{:T(128)}, f32[8,128,1024]{2,1,0:T(8,128)}, ...), condition=%wide.region_8.9_spmd, body=%wide.region_1.8_spmd.sunk | while | flops 405146720 | bytes 29779532 | solution.py:104
  22.7 4.3 scatter_fusion.1
  27.5 4.3 scatter_fusion
  41.0 4.2 scatter_fusion.1
  45.7 4.3 scatter_fusion
  52.5 6.8 %add.427 = f32[8,128,1024]{2,1,0:T(8,128)} add(f32[8,128,1024]{2,1,0:T(8,128)} %get-tuple-element.699, f32[8,128,1024]{2,1,0:T(8,128)} %get-tuple-element.700) | non-fusion elementwise | flops 1048576 | bytes 12582912 | tf_op jit(solution)/shard_map/add | solution.py:108
  61.8 18.0 %while.105 = (s32[]{:T(128)}, f32[8,128,1024]{2,1,0:T(8,128)}, f32[8,128]{1,0:T(8,128)S(1)}, f32[8,128,1024]{2,1,0:T(8,128)}, f32[8,128]{1,0:T(8,128)S(1)}, /*in...) while((s32[]{:T(128)}, f32[8,128,1024]{2,1,0:T(8,128)}, ...), condition=%wide.region_16.17_spmd, body=%wide.region_9.16_spmd.sunk | while | flops 405146688 | bytes 29779436 | solution.py:104
  69.8 4.3 scatter_fusion.3
  87.4 23.2 %collective-permute-done.2 = bf16[8,128]{1,0:T(8,128)(2,1)S(1)} collective-permute-done((bf16[8,128]{1,0:T(8,128)(2,1)S(1)}, bf16[8,128]{1,0:T(8,128)(2,1)S(1)}, u32[]{:S(2)}, u32[]{:S(2)}) %collective-permute-start.2) | collective-permute-done | bytes 2080 | tf_op jit(solution)/shard_map/ppermute | solution.py:16
  110.6 5.2 convert_add_fusion.3
  115.8 48.7 %collective-permute-done.3 = bf16[8,128,1024]{2,1,0:T(8,128)(2,1)} collective-permute-done((bf16[8,128,1024]{2,1,0:T(8,128)(2,1)}, bf16[8,128,1024]{2,1,0:T(8,128)(2,1)}, u32[]{:S(2)}, u32[]{:S(2)}) %collective-permute-start.3) | collective-permute-done | bytes 2097184 | tf_op jit(solution)/shard_map/ppermute | solution.py:16
  167.0 17.8 %while.106 = (s32[]{:T(128)}, f32[8,128,1024]{2,1,0:T(8,128)}, f32[8,128]{1,0:T(8,128)S(1)}, f32[8,128,1024]{2,1,0:T(8,128)}, f32[8,128]{1,0:T(8,128)S(1)}, /*in...) while((s32[]{:T(128)}, f32[8,128,1024]{2,1,0:T(8,128)}, ...), condition=%wide.region_24.25_spmd, body=%wide.region_17.24_spmd.sunk | while | flops 405146688 | bytes 29779436 | solution.py:104
  174.8 4.1 scatter_fusion.5
  179.3 4.1 scatter_fusion.4
  190.1 4.3 gather_fusion.10
  194.4 4.4 gather_fusion.11
  201.4 7.5 %pad_maximum_fusion = bf16[16,2,128,1024]{3,2,1,0:T(8,128)(2,1)} fusion(bf16[16,1,128,1024]{3,2,1,0:T(8,128)(2,1)} %bitcast.209, bf16[16,1,128,1024]{3,2,1,0:T(8,128)(2,1)} %bitcast.208), kind=kLoop, calls=%fused_computation.173 | loop fusion | flops 4194304 | bytes 16777216 | tf_op jit(solution)/shard_map/stack | solution.py:120
  209.6 74.9 %collective-permute-done.5 = bf16[8,128]{1,0:T(8,128)(2,1)S(1)} collective-permute-done((bf16[8,128]{1,0:T(8,128)(2,1)S(1)}, bf16[8,128]{1,0:T(8,128)(2,1)S(1)}, u32[]{:S(2)}, u32[]{:S(2)}) %collective-permute-start.5) | collective-permute-done | bytes 2080 | tf_op jit(solution)/shard_map/ppermute | solution.py:16
  284.5 5.2 convert_add_fusion.2
  292.3 15.2 %collective-permute-start.8 = (bf16[8,128]{1,0:T(8,128)(2,1)S(1)}, bf16[8,128]{1,0:T(8,128)(2,1)S(1)}, u32[]{:S(2)}, u32[]{:S(2)}) collective-permute-start(bf16[8,128]{1,0:T(8,128)(2,1)S(1)} %convert_element_type.254), channel_id=1, source_target_pairs={{5,0},{6,1},{7,2},{0,3},{1,4},{2,5},{3,6},{4,7},{13,8},{14,9},{15,... | collective-permute-start | bytes 6152 | tf_op jit(solution)/shard_map/ppermute | solution.py:16
  311.4 22.2 %collective-permute-start.7 = (bf16[8,128,1024]{2,1,0:T(8,128)(2,1)}, bf16[8,128,1024]{2,1,0:T(8,128)(2,1)S(1)}, u32[]{:S(2)}, u32[]{:S(2)}) collective-permute-start(bf16[8,128,1024]{2,1,0:T(8,128)(2,1)} %convert_element_type.252), channel_id=1, source_target_pairs={{5,0},{6,1},{7,2},{0,3},{1,4},{2,5},{3,6},{4,7},{13,8},{14,9},{15,... | collective-permute-start | bytes 6291464 | tf_op jit(solution)/shard_map/ppermute | solution.py:16
  333.6 73.9 %while.109 = (s32[]{:T(128)}, bf16[16,2,128,1024]{3,2,1,0:T(8,128)(2,1)}, bf16[16,2,128]{2,1,0:T(2,128)(2,1)S(1)}, bf16[16,2,128,1024]{3,2,1,0:T(8,128)(2,1)}, s32[]{:T(128)}, /*index=5*/s32[]{:T(128)}, s32[]{}) while((s32[]{:T(128)}, bf16[16,2,128,1024]{3,2,1,0:T(8,128)(2,1)}, bf16[16,2,128]{2,1,0:T(2,128)(2,1)S(1)}, ...), condition=%wide.region_44.45_spmd, body=%wide.region_41.44_spmd.sunk | while | flops 102073088 | bytes 2724453 | solution.py:53
  408.1 5.3 convert_add_fusion.1
  415.9 18.0 %while.108 = (s32[]{:T(128)}, f32[8,128,1024]{2,1,0:T(8,128)}, f32[8,128]{1,0:T(8,128)S(1)}, f32[8,128,1024]{2,1,0:T(8,128)}, f32[8,128]{1,0:T(8,128)S(1)}, /*in...) while((s32[]{:T(128)}, f32[8,128,1024]{2,1,0:T(8,128)}, ...), condition=%wide.region_40.41_spmd, body=%wide.region_33.40_spmd.sunk | while | flops 405146688 | bytes 29779436 | solution.py:104
  423.8 4.4 scatter_fusion.9
  437.7 11.7 %convert_multiply_fusion = f32[16,2,128,1024]{3,2,1,0:T(8,128)} fusion(bf16[16,2,128,1024]{3,2,1,0:T(8,128)(2,1)} %get-tuple-element.717, f32[16]{0:T(128)S(1)} %get-tuple-element.876), kind=kLoop, calls=%fused_computation.170 | loop fusion | flops 8388608 | bytes 25165888 | tf_op jit(solution)/shard_map/mul | solution.py:122
  449.5 10.9 %slice_bitcast_fusion = (f32[16,128,1024]{2,1,0:T(8,128)}, f32[16,128,1024]{2,1,0:T(8,128)}) fusion(f32[16,2,128,1024]{3,2,1,0:T(8,128)} %convert_multiply_fusion), kind=kLoop, calls=%fused_computation.171 | loop fusion | bytes 33554432 | tf_op jit(solution)/shard_map/squeeze | solution.py:124
  463.9 23.6 %collective-permute-done.11 = bf16[8,128]{1,0:T(8,128)(2,1)S(1)} collective-permute-done((bf16[8,128]{1,0:T(8,128)(2,1)S(1)}, bf16[8,128]{1,0:T(8,128)(2,1)S(1)}, u32[]{:S(2)}, u32[]{:S(2)}) %collective-permute-start.11) | collective-permute-done | bytes 2080 | tf_op jit(solution)/shard_map/ppermute | solution.py:16
  489.7 5.2 convert_add_fusion
  494.8 16.9 %scatter_fusion.10 = f32[8,128,1024]{2,1,0:T(8,128)} fusion(f32[8,128,1024]{2,1,0:T(8,128)} %convert_add_fusion, s32[16]{0:T(128)S(1)} %get-tuple-element.878, f32[16,128,1024]{2,1,0:T(8,128)} %get-tuple-element.868), kind=kCustom, calls=%fused_computation.32 | custom fusion | flops 2097152 | bytes 25165888 | tf_op jit(solution)/shard_map/scatter-add | solution.py:124
  511.8 17.9 %scatter_fusion.11 = f32[8,128,1024]{2,1,0:T(8,128)} fusion(f32[8,128,1024]{2,1,0:T(8,128)} %scatter_fusion.10, s32[16]{0:T(128)S(1)} %get-tuple-element.877, f32[16,128,1024]{2,1,0:T(8,128)} %get-tuple-element.867), kind=kCustom, calls=%fused_computation.33 | custom fusion | flops 2097152 | bytes 25165888 | tf_op jit(solution)/shard_map/scatter-add | solution.py:124
  529.7 5.1 subtract_convert_fusion
  (216 shorter events, 181.8 us)
Async XLA Ops:
  0.6 7.9 %copy-start.6 = (s32[1,1,5]{2,1,0:T(1,128)S(1)}, s32[1,1,5]{2,1,0:T(1,128)}, u32[]{:S(2)}) copy-start(s32[1,1,5]{2,1,0:T(1,128)} %param.18) | copy-start | bytes 64
  0.6 9.2 %copy-start.7 = (s32[1,1,5,64,2]{3,4,2,1,0:T(2,128)S(1)}, s32[1,1,5,64,2]{3,4,2,1,0:T(2,128)}, u32[]{:S(2)}) copy-start(s32[1,1,5,64,2]{3,4,2,1,0:T(2,128)} %param.17) | copy-start | bytes 7684
  6.1 53.2 %collective-permute-start = (bf16[8,128,1024]{2,1,0:T(8,128)(2,1)}, bf16[8,128,1024]{2,1,0:T(8,128)(2,1)}, u32[]{:S(2)}, u32[]{:S(2)}) collective-permute-start(bf16[8,128,1024]{2,1,0:T(8,128)(2,1)} %bitcast.18), channel_id=1, source_target_pairs={{1,0},{2,1},{3,2},{4,3},{5,4},{6,5},{7,6},{0,7},{9,8},{10,9},{11,1... | collective-permute-start | bytes 6291464 | tf_op jit(solution)/shard_map/ppermute | solution.py:16
  19.9 1.1 copy-start
  38.2 1.1 copy-start
  66.3 1.1 copy-start.1
  83.7 26.9 %collective-permute-start.1 = (bf16[8,128,1024]{2,1,0:T(8,128)(2,1)}, bf16[8,128,1024]{2,1,0:T(8,128)(2,1)S(1)}, u32[]{:S(2)}, u32[]{:S(2)}) collective-permute-start(bf16[8,128,1024]{2,1,0:T(8,128)(2,1)} %convert_element_type.244), channel_id=1, source_target_pairs={{7,0},{0,1},{1,2},{2,3},{3,4},{4,5},{5,6},{6,7},{15,8},{8,9},{9,10... | collective-permute-start | bytes 6291464 | tf_op jit(solution)/shard_map/ppermute | solution.py:16
  83.7 80.8 %collective-permute-start.3 = (bf16[8,128,1024]{2,1,0:T(8,128)(2,1)}, bf16[8,128,1024]{2,1,0:T(8,128)(2,1)}, u32[]{:S(2)}, u32[]{:S(2)}) collective-permute-start(bf16[8,128,1024]{2,1,0:T(8,128)(2,1)} %bitcast.18), channel_id=1, source_target_pairs={{2,0},{3,1},{4,2},{5,3},{6,4},{7,5},{0,6},{1,7},{10,8},{11,9},{12,... | collective-permute-start | bytes 6291464 | tf_op jit(solution)/shard_map/ppermute | solution.py:16
  84.4 26.2 %collective-permute-start.2 = (bf16[8,128]{1,0:T(8,128)(2,1)S(1)}, bf16[8,128]{1,0:T(8,128)(2,1)S(1)}, u32[]{:S(2)}, u32[]{:S(2)}) collective-permute-start(bf16[8,128]{1,0:T(8,128)(2,1)S(1)} %convert_element_type.246), channel_id=1, source_target_pairs={{7,0},{0,1},{1,2},{2,3},{3,4},{4,5},{5,6},{6,7},{15,8},{8,9},{9,10... | collective-permute-start | bytes 6152 | tf_op jit(solution)/shard_map/ppermute | solution.py:16
  171.5 1.0 copy-start.2
  184.8 5.3 copy-start.8
  188.6 95.9 %collective-permute-start.4 = (bf16[8,128,1024]{2,1,0:T(8,128)(2,1)}, bf16[8,128,1024]{2,1,0:T(8,128)(2,1)S(1)}, u32[]{:S(2)}, u32[]{:S(2)}) collective-permute-start(bf16[8,128,1024]{2,1,0:T(8,128)(2,1)} %convert_element_type.248), channel_id=1, source_target_pairs={{6,0},{7,1},{0,2},{1,3},{2,4},{3,5},{4,6},{5,7},{14,8},{15,9},{8,1... | collective-permute-start | bytes 6291464 | tf_op jit(solution)/shard_map/ppermute | solution.py:16
  188.6 101.2 %collective-permute-start.6 = (bf16[8,128,1024]{2,1,0:T(8,128)(2,1)}, bf16[8,128,1024]{2,1,0:T(8,128)(2,1)}, u32[]{:S(2)}, u32[]{:S(2)}) collective-permute-start(bf16[8,128,1024]{2,1,0:T(8,128)(2,1)} %bitcast.18), channel_id=1, source_target_pairs={{3,0},{4,1},{5,2},{6,3},{7,4},{0,5},{1,6},{2,7},{11,8},{12,9},{13,... | collective-permute-start | bytes 6291464 | tf_op jit(solution)/shard_map/ppermute | solution.py:16
  188.8 224.6 %collective-permute-start.9 = (bf16[8,128,1024]{2,1,0:T(8,128)(2,1)}, bf16[8,128,1024]{2,1,0:T(8,128)(2,1)}, u32[]{:S(2)}, u32[]{:S(2)}) collective-permute-start(bf16[8,128,1024]{2,1,0:T(8,128)(2,1)} %bitcast.18), channel_id=1, source_target_pairs={{4,0},{5,1},{6,2},{7,3},{0,4},{1,5},{2,6},{3,7},{12,8},{13,9},{14,... | collective-permute-start | bytes 6291464 | tf_op jit(solution)/shard_map/ppermute | solution.py:16
  198.8 85.7 %collective-permute-start.5 = (bf16[8,128]{1,0:T(8,128)(2,1)S(1)}, bf16[8,128]{1,0:T(8,128)(2,1)S(1)}, u32[]{:S(2)}, u32[]{:S(2)}) collective-permute-start(bf16[8,128]{1,0:T(8,128)(2,1)S(1)} %convert_element_type.250), channel_id=1, source_target_pairs={{6,0},{7,1},{0,2},{1,3},{2,4},{3,5},{4,6},{5,7},{14,8},{15,9},{8,1... | collective-permute-start | bytes 6152 | tf_op jit(solution)/shard_map/ppermute | solution.py:16
  292.3 115.9 %collective-permute-start.8 = (bf16[8,128]{1,0:T(8,128)(2,1)S(1)}, bf16[8,128]{1,0:T(8,128)(2,1)S(1)}, u32[]{:S(2)}, u32[]{:S(2)}) collective-permute-start(bf16[8,128]{1,0:T(8,128)(2,1)S(1)} %convert_element_type.254), channel_id=1, source_target_pairs={{5,0},{6,1},{7,2},{0,3},{1,4},{2,5},{3,6},{4,7},{13,8},{14,9},{15,... | collective-permute-start | bytes 6152 | tf_op jit(solution)/shard_map/ppermute | solution.py:16
  311.4 96.7 %collective-permute-start.7 = (bf16[8,128,1024]{2,1,0:T(8,128)(2,1)}, bf16[8,128,1024]{2,1,0:T(8,128)(2,1)S(1)}, u32[]{:S(2)}, u32[]{:S(2)}) collective-permute-start(bf16[8,128,1024]{2,1,0:T(8,128)(2,1)} %convert_element_type.252), channel_id=1, source_target_pairs={{5,0},{6,1},{7,2},{0,3},{1,4},{2,5},{3,6},{4,7},{13,8},{14,9},{15,... | collective-permute-start | bytes 6291464 | tf_op jit(solution)/shard_map/ppermute | solution.py:16
  413.4 2.5 copy-start.5
  420.5 1.0 copy-start.4
  437.7 51.9 %collective-permute-start.10 = (bf16[8,128,1024]{2,1,0:T(8,128)(2,1)}, bf16[8,128,1024]{2,1,0:T(8,128)(2,1)S(1)}, u32[]{:S(2)}, u32[]{:S(2)}) collective-permute-start(bf16[8,128,1024]{2,1,0:T(8,128)(2,1)} %convert_element_type.256), channel_id=1, source_target_pairs={{4,0},{5,1},{6,2},{7,3},{0,4},{1,5},{2,6},{3,7},{12,8},{13,9},{14,... | collective-permute-start | bytes 6291464 | tf_op jit(solution)/shard_map/ppermute | solution.py:16
  460.4 27.1 %collective-permute-start.11 = (bf16[8,128]{1,0:T(8,128)(2,1)S(1)}, bf16[8,128]{1,0:T(8,128)(2,1)S(1)}, u32[]{:S(2)}, u32[]{:S(2)}) collective-permute-start(bf16[8,128]{1,0:T(8,128)(2,1)S(1)} %convert_element_type.261), channel_id=1, source_target_pairs={{4,0},{5,1},{6,2},{7,3},{0,4},{1,5},{2,6},{3,7},{12,8},{13,9},{14,... | collective-permute-start | bytes 6152 | tf_op jit(solution)/shard_map/ppermute | solution.py:16
where the time goes:
time: 537 us; the launch traced here: 535 us
  other arithmetic  176 us (33%)
  waiting for transfers between devices  170 us (32%)
  matrix products  72.9 us (14%)
  local copies, waits for them, and re-layouts  60.3 us (11%)
  starting transfers between devices  50.6 us (9%)
    ppermute x12, waiting for transfers between devices, passed_along(): return lax.ppermute(block, axis, route)  170 us
    ppermute x12, starting transfers between devices, passed_along(): return lax.ppermute(block, axis, route)  50.6 us
    scatter-add x2, other arithmetic, shards(): near_sums.at[first_ids].add(tile_sums[:, 0]).at[second_ids]  34.9 us
    dot_general x21, matrix products, pair_terms(): jnp.einsum('nij,nid->njd', kernel_low, first_block, preferred_element_typ...  27.7 us
    dot_general x21, matrix products, pair_terms(): jnp.einsum('nid,njd->nij', first_block, second_block, preferred_element_t...  24.3 us
    scatter-add x5, other arithmetic, step(): far_sums.at[second_ids].add(to_second * other_mask[:, None, None])  21.3 us
    add x4, other arithmetic, shards(): near_sums = near_sums + back_sums.astype(jnp.float32)  20.9 us
    dot_general x21, matrix products, pair_terms(): jnp.einsum('nij,njd->nid', kernel_low, second_block, preferred_element_ty...  20.9 us
  transfers between devices with their start and end apart: 12, of which 4 were waited for; matrix products, arithmetic and copies ran while one was open for 35% of the time, Pallas kernels for 0%

commit v1 on v0

v1 whole, which is shorter than its diff:
```python
import functools

import jax
import jax.numpy as jnp
from jax import lax
from jax.experimental import pallas as pl
from jax.experimental.pallas import tpu as pltpu
from jax.sharding import PartitionSpec as P

BLOCK = 128
sharpness = 4.0
epsilon = 1e-06
VMEM_BYTES = 56 * 2**20
CHIPS = 4


def along_chips(x, hops):
    route = [(o, ((o // 2 + hops) % CHIPS) * 2 + o % 2) for o in range(2 * CHIPS)]
    return lax.ppermute(x, "owner", route)


def to_sibling(x):
    return lax.ppermute(x, "owner", [(o, o ^ 1) for o in range(2 * CHIPS)])


def normalize_kernel(x_ref, u_ref):
    wide = x_ref[...].astype(jnp.float32)
    mean = jnp.mean(wide * wide, axis=-1, keepdims=True)
    u_ref[...] = (wide * lax.rsqrt(mean + epsilon)).astype(jnp.bfloat16)


def normalize(x):
    rows, width = x.shape
    step = 256
    return pl.pallas_call(
        normalize_kernel,
        grid=(rows // step,),
        in_specs=[pl.BlockSpec((step, width), lambda i: (i, 0))],
        out_specs=pl.BlockSpec((step, width), lambda i: (i, 0)),
        out_shape=jax.ShapeDtypeStruct(x.shape, jnp.bfloat16),
        compiler_params=pltpu.CompilerParams(vmem_limit_bytes=VMEM_BYTES),
        name="normalize",
    )(x)


def rows_of(block):
    return pl.ds(pl.multiple_of(block * BLOCK, BLOCK), BLOCK)


def add_terms(u_ref, q_ref, acc_ref, kacc_ref, mine, other):
    p = u_ref[rows_of(mine), :]
    q = q_ref[rows_of(other), :]
    dots = lax.dot_general(p, q, (((1,), (1,)), ((), ())), preferred_element_type=jnp.float32)
    kernel = jnp.exp(sharpness * (dots * (1.0 / q.shape[1]) - 1.0))
    kacc_ref[rows_of(mine), :] += kernel
    acc_ref[rows_of(mine), :] += jnp.dot(
        kernel.astype(jnp.bfloat16), q, preferred_element_type=jnp.float32
    )


def own_kernel(list_ref, surplus_ref, u_ref, acc_ref, kacc_ref):
    acc_ref[...] = jnp.zeros_like(acc_ref)
    kacc_ref[...] = jnp.zeros_like(kacc_ref)

    def both(a, b):
        add_terms(u_ref, u_ref, acc_ref, kacc_ref, a, b)

        @pl.when(a != b)
        def _():
            add_terms(u_ref, u_ref, acc_ref, kacc_ref, b, a)

    def home(t, carry):
        both(list_ref[0, 2 * t], list_ref[0, 2 * t + 1])
        return carry

    lax.fori_loop(0, list_ref[0, 128], home, 0)

    def surplus(t, carry):
        @pl.when(surplus_ref[t, 2] == 1)
        def _():
            both(surplus_ref[t, 0], surplus_ref[t, 1])

        return carry

    lax.fori_loop(0, surplus_ref.shape[0], surplus, 0)


def run_lists(core_ref, list_ref, rows, buffers, u_ref, acc_ref, kacc_ref):
    for (row0, row1), q_ref in zip(rows, buffers):
        row = jnp.where(core_ref[0] == 0, row0, row1)

        def step(t, carry):
            add_terms(u_ref, q_ref, acc_ref, kacc_ref, list_ref[row, 2 * t], list_ref[row, 2 * t + 1])
            return carry

        lax.fori_loop(0, list_ref[row, 128], step, 0)


def far_kernel(rows, core_ref, list_ref, u_ref, acc_in, kacc_in, *refs):
    buffers, (acc_ref, kacc_ref) = refs[:-2], refs[-2:]
    acc_ref[...] = acc_in[...]
    kacc_ref[...] = kacc_in[...]
    run_lists(core_ref, list_ref, rows, buffers, u_ref, acc_ref, kacc_ref)


def last_kernel(rows, core_ref, list_ref, u_ref, acc_in, kacc_in, *refs):
    buffers, (out_ref, log_ref, acc_ref, kacc_ref) = refs[:-4], refs[-4:]
    acc_ref[...] = acc_in[...]
    kacc_ref[...] = kacc_in[...]
    run_lists(core_ref, list_ref, rows, buffers, u_ref, acc_ref, kacc_ref)
    for block in range(out_ref.shape[0] // BLOCK):
        here = slice(block * BLOCK, (block + 1) * BLOCK)
        kernel = kacc_ref[here, :]
        density = jnp.sum(kernel, axis=1, keepdims=True)
        out_ref[here, :] = (
            u_ref[here, :].astype(jnp.float32) - acc_ref[here, :] / density
        ).astype(jnp.bfloat16)
        log_ref[block : block + 1, :] = jnp.log(jnp.sum(kernel.T, axis=0, keepdims=True))


SMEM = pl.BlockSpec(memory_space=pltpu.SMEM)
VMEM = pl.BlockSpec(memory_space=pltpu.VMEM)


def params():
    return pltpu.CompilerParams(vmem_limit_bytes=VMEM_BYTES)


def cost(pairs, width):
    return pl.CostEstimate(
        flops=pairs * 4 * BLOCK * BLOCK * width, bytes_accessed=8 * 2**20, transcendentals=pairs * BLOCK * BLOCK
    )


def shards(embeddings, home_pairs, home_count, surplus_pairs):
    rows, width = embeddings.shape
    pairs, count = home_pairs[0, 0], home_count[0, 0]
    shifts = pairs.shape[0]

    def table(listed):
        return jnp.concatenate(
            [listed.reshape(shifts, -1), count[:, None], jnp.zeros((shifts, 7), jnp.int32)], axis=1
        )

    mine = table(pairs)
    turned = table(pairs[:, :, ::-1])
    owners = 2 * CHIPS
    theirs = [
        lax.ppermute(turned[s : s + 1], "owner", [(o, (o + s) % owners) for o in range(owners)])
        for s in range(1, shifts)
    ]
    lists = jnp.concatenate([mine] + theirs, axis=0)
    core = (lax.axis_index("owner") % 2).astype(jnp.int32).reshape(1)

    unit = normalize(embeddings)
    half = rows // 2
    low, high = unit[:half], unit[half:]
    b_low, a_high = along_chips(low, 1), along_chips(high, -1)
    b_high, a_low = along_chips(high, 1), along_chips(low, -1)
    sib = to_sibling(unit)
    o_low, o_high = along_chips(b_low, 1), along_chips(a_high, -1)

    below = jnp.concatenate([b_low, b_high], axis=0)
    above = jnp.concatenate([a_low, a_high], axis=0)
    below_x, above_x = to_sibling(below), to_sibling(above)
    opposite = jnp.concatenate([o_low, o_high], axis=0)
    opposite_x = to_sibling(opposite)

    sums = (
        jax.ShapeDtypeStruct((rows, width), jnp.float32),
        jax.ShapeDtypeStruct((rows, BLOCK), jnp.float32),
    )
    acc, kacc = pl.pallas_call(
        own_kernel,
        in_specs=[SMEM, SMEM, VMEM],
        out_specs=(VMEM, VMEM),
        out_shape=sums,
        compiler_params=params(),
        cost_estimate=cost(64, width),
        name="own_pairs",
    )(mine, surplus_pairs[0, 0], unit)

    acc, kacc = pl.pallas_call(
        functools.partial(far_kernel, ((1, 5), (2, 2), (3, 1), (6, 6), (5, 7))),
        in_specs=[SMEM, SMEM] + [VMEM] * 8,
        out_specs=(VMEM, VMEM),
        out_shape=sums,
        compiler_params=params(),
        cost_estimate=cost(12, width),
        name="near_pairs",
    )(core, lists, unit, acc, kacc, sib, above, above_x, below, below_x)

    centered, log_density = pl.pallas_call(
        functools.partial(last_kernel, ((4, 4), (8, 8), (7, 3))),
        in_specs=[SMEM, SMEM] + [VMEM] * 6,
        out_specs=(VMEM, VMEM),
        out_shape=(
            jax.ShapeDtypeStruct((rows, width), jnp.bfloat16),
            jax.ShapeDtypeStruct((rows // BLOCK, BLOCK), jnp.float32),
        ),
        scratch_shapes=[pltpu.VMEM((rows, width), jnp.float32), pltpu.VMEM((rows, BLOCK), jnp.float32)],
        compiler_params=params(),
        cost_estimate=cost(8, width),
        name="opposite_pairs",
    )(core, lists, unit, acc, kacc, opposite, opposite, opposite_x)
    return centered, log_density.reshape(rows)


def solution(mesh):
    return jax.shard_map(
        shards,
        mesh=mesh,
        in_specs=(
            P(("group", "owner"), None),
            P("group", "owner", None, None, None),
            P("group", "owner", None),
            P("group", "owner", None, None),
        ),
        out_specs=(P(("group", "owner"), None), P(("group", "owner"))),
        check_vma=False,
    )
```

time: 537 us -> 155 us (0.29)
  the two profiles are of different devices: /device:TPU:102 before, /device:TPU:1 now
where the time goes in v1:
time: 155 us
  waiting for transfers between devices  58.7 us (38%)
  starting transfers between devices  49.8 us (32%)
  Pallas kernels  34.1 us (22%)
  local copies, waits for them, and re-layouts  10.7 us (7%)
    ppermute x6, waiting for transfers between devices, along_chips(): return lax.ppermute(x, 'owner', route)  52.7 us
    ppermute x4, starting transfers between devices, shards(): lax.ppermute(turned[s:s + 1], 'owner', [(o, (o + s) % owners) for o in ra...  34.1 us
    pallas_call x1, Pallas kernels, shards(): pl.pallas_call(functools.partial(far_kernel, ((1, 5), (2, 2), (3, 1), (6,...  13.1 us
    pallas_call x1, Pallas kernels, shards(): pl.pallas_call(own_kernel, in_specs=[SMEM, SMEM, VMEM], out_specs=(VMEM,...  9.51 us
    ppermute x6, starting transfers between devices, along_chips(): return lax.ppermute(x, 'owner', route)  9.07 us
    pallas_call x1, Pallas kernels, shards(): pl.pallas_call(functools.partial(last_kernel, ((4, 4), (8, 8), (7, 3))),...  7.26 us
    ppermute x4, starting transfers between devices, to_sibling(): return lax.ppermute(x, 'owner', [(o, o ^ 1) for o in range(2 * CHIPS)])  6.7 us
    ppermute x4, waiting for transfers between devices, shards(): lax.ppermute(turned[s:s + 1], 'owner', [(o, (o + s) % owners) for o in ra...  5.94 us
  transfers between devices with their start and end apart: 14, of which 6 were waited for; matrix products, arithmetic and copies ran while one was open for 6% of the time, Pallas kernels for 15%

profile of v1, /device:TPU:1, one launch (start us, length us, event | category | flops | bytes accessed | tf_op | source)
XLA Modules:
  0.0 154.6 jit_solution(9732973456491023316)
XLA Ops:
  0.6 4.2 %normalize.1.u_ref = bf16[1024,1024]{1,0:T(8,128)(2,1)} custom-call(bf16[1024,1024]{1,0:T(8,128)(2,1)} %x_ref.1), custom_call_target="tpu_custom_call" | custom-call | tf_op jit(solution)/shard_map/normalize/pallas_call | solution.py:35
  4.8 1.9 %fusion.2 = (bf16[512,1024]{1,0:T(8,128)(2,1)S(1)}, bf16[512,1024]{1,0:T(8,128)(2,1)S(1)}) fusion(bf16[1024,1024]{1,0:T(8,128)(2,1)} %normalize.1.u_ref), kind=kLoop, calls=%fused_computation.10 | loop fusion | bytes 4194304 | tf_op jit(solution)/shard_map/slice | solution.py:157
  6.7 2.2 %collective-permute-start.8 = (bf16[512,1024]{1,0:T(8,128)(2,1)S(1)}, bf16[512,1024]{1,0:T(8,128)(2,1)S(1)}, u32[]{:S(2)}, u32[]{:S(2)}) collective-permute-start(bf16[512,1024]{1,0:T(8,128)(2,1)S(1)} %get-tuple-element.15), channel_id=1, source_target_pairs={{0,2},{1,3},{2,4},{3,5},{4,6},{5,7},{6,0},{7,1},{8,10},{9,11},{10,... | collective-permute-start | bytes 3145736 | tf_op jit(solution)/shard_map/ppermute | solution.py:19
  8.9 1.5 collective-permute-start.6
  10.4 2.7 %collective-permute-start.5 = (bf16[512,1024]{1,0:T(8,128)(2,1)S(1)}, bf16[512,1024]{1,0:T(8,128)(2,1)S(1)}, u32[]{:S(2)}, u32[]{:S(2)}) collective-permute-start(bf16[512,1024]{1,0:T(8,128)(2,1)S(1)} %get-tuple-element.15), channel_id=1, source_target_pairs={{0,6},{1,7},{2,0},{3,1},{4,2},{5,3},{6,4},{7,5},{8,14},{9,15},{10,... | collective-permute-start | bytes 3145736 | tf_op jit(solution)/shard_map/ppermute | solution.py:19
  13.1 20.0 %collective-permute-done.8 = bf16[512,1024]{1,0:T(8,128)(2,1)S(1)} collective-permute-done((bf16[512,1024]{1,0:T(8,128)(2,1)S(1)}, bf16[512,1024]{1,0:T(8,128)(2,1)S(1)}, u32[]{:S(2)}, u32[]{:S(2)}) %collective-permute-start.8) | collective-permute-done | bytes 1048608 | tf_op jit(solution)/shard_map/ppermute | solution.py:19
  33.1 2.7 %collective-permute-start.12 = (bf16[512,1024]{1,0:T(8,128)(2,1)S(1)}, bf16[512,1024]{1,0:T(8,128)(2,1)S(1)}, u32[]{:S(2)}, u32[]{:S(2)}) collective-permute-start(bf16[512,1024]{1,0:T(8,128)(2,1)S(1)} %collective-permute-done.6), channel_id=1, source_target_pairs={{0,6},{1,7},{2,0},{3,1},{4,2},{5,3},{6,4},{7,5},{8,14},{9,15},{10,... | collective-permute-start | bytes 3145736 | tf_op jit(solution)/shard_map/ppermute | solution.py:19
  35.7 2.9 %collective-permute-start.4 = (bf16[1024,1024]{1,0:T(8,128)(2,1)S(1)}, bf16[1024,1024]{1,0:T(8,128)(2,1)}, u32[]{:S(2)}, u32[]{:S(2)}) collective-permute-start(bf16[1024,1024]{1,0:T(8,128)(2,1)S(1)} %copy-done), channel_id=1, source_target_pairs={{0,1},{1,0},{2,3},{3,2},{4,5},{5,4},{6,7},{7,6},{8,9},{9,8},{10,11... | collective-permute-start | bytes 6291464 | tf_op jit(solution)/shard_map/ppermute | solution.py:23
  38.7 1.1 constant_dynamic-update-slice_fusion.3
  39.8 15.8 %collective-permute-done.9 = bf16[512,1024]{1,0:T(8,128)(2,1)S(1)} collective-permute-done((bf16[512,1024]{1,0:T(8,128)(2,1)S(1)}, bf16[512,1024]{1,0:T(8,128)(2,1)S(1)}, u32[]{:S(2)}, u32[]{:S(2)}) %collective-permute-start.9) | collective-permute-done | bytes 1048608 | tf_op jit(solution)/shard_map/ppermute | solution.py:19
  55.5 1.0 constant_dynamic-update-slice_fusion.2.refs_3_
  56.6 2.4 %collective-permute-start.10 = (bf16[1024,1024]{1,0:T(8,128)(2,1)}, bf16[1024,1024]{1,0:T(8,128)(2,1)}, u32[]{:S(2)}, u32[]{:S(2)}) collective-permute-start(bf16[1024,1024]{1,0:T(8,128)(2,1)} %constant_dynamic-update-slice_fusion.2.refs_3_), channel_id=1, source_target_pairs={{0,1},{1,0},{2,3},{3,2},{4,5},{5,4},{6,7},{7,6},{8,9},{9,8},{10,11... | collective-permute-start | bytes 6291464 | tf_op jit(solution)/shard_map/ppermute | solution.py:23
  58.9 1.0 constant_dynamic-update-slice_fusion.1
  60.0 1.0 constant_dynamic-update-slice_fusion.refs_1_
  61.0 17.0 %collective-permute-done.11 = bf16[512,1024]{1,0:T(8,128)(2,1)S(1)} collective-permute-done((bf16[512,1024]{1,0:T(8,128)(2,1)S(1)}, bf16[512,1024]{1,0:T(8,128)(2,1)S(1)}, u32[]{:S(2)}, u32[]{:S(2)}) %collective-permute-start.11) | collective-permute-done | bytes 1048608 | tf_op jit(solution)/shard_map/ppermute | solution.py:19
  78.0 1.1 constant_dynamic-update-slice_fusion.5
  79.1 1.0 constant_dynamic-update-slice_fusion.4.refs_0_.refs_1_
  80.1 1.4 collective-permute-start.13
  81.7 0.1 copy.14
  82.1 0.6 fusion.1
  82.7 0.1 collective-permute-start
  82.9 2.3 %collective-permute-done = s32[1,136]{1,0:T(1,128)S(1)} collective-permute-done((s32[1,136]{1,0:T(1,128)S(1)}, s32[1,136]{1,0:T(1,128)S(1)}, u32[]{:S(2)}, u32[]{:S(2)}) %collective-permute-start) | collective-permute-done | bytes 576 | tf_op jit(solution)/shard_map/ppermute | solution.py:149
  85.1 0.2 collective-permute-start.1
  85.4 0.7 copy.18
  86.1 2.7 %collective-permute-done.1 = s32[1,136]{1,0:T(1,128)S(1)} collective-permute-done((s32[1,136]{1,0:T(1,128)S(1)}, s32[1,136]{1,0:T(1,128)S(1)}, u32[]{:S(2)}, u32[]{:S(2)}) %collective-permute-start.1) | collective-permute-done | bytes 576 | tf_op jit(solution)/shard_map/ppermute | solution.py:149
  88.8 2.1 %collective-permute-start.2 = (s32[1,136]{1,0:T(1,128)S(1)}, s32[1,136]{1,0:T(1,128)S(1)}, u32[]{:S(2)}, u32[]{:S(2)}) collective-permute-start(s32[1,136]{1,0:T(1,128)S(1)} %get-tuple-element.17), channel_id=1, source_target_pairs={{0,3},{1,4},{2,5},{3,6},{4,7},{5,0},{6,1},{7,2},{8,11},{9,12},{10,... | collective-permute-start | bytes 1640 | tf_op jit(solution)/shard_map/ppermute | solution.py:149
  90.8 9.5 %own_pairs.1 = (f32[1024,1024]{1,0:T(8,128)}, f32[1024,128]{1,0:T(8,128)}) custom-call(s32[5,136]{1,0:T(8,128)} %get-tuple-element.21.list_ref, s32[16,3]{1,0:T(8,128)} %bitcast.10, bf16[1024,1024]{1,0:T(8,128)(2,1)} %normalize.1.u_ref), custom_call_target="tpu_custom_call" | custom-call | flops 4294967296 | bytes 8388608 | tf_op jit(solution)/shard_map/own_pairs/pallas_call | solution.py:173
  100.4 31.6 %collective-permute-start.3 = (s32[1,136]{1,0:T(1,128)S(1)}, s32[1,136]{1,0:T(1,128)S(1)}, u32[]{:S(2)}, u32[]{:S(2)}) collective-permute-start(s32[1,136]{1,0:T(1,128)S(1)} %get-tuple-element.16), channel_id=1, source_target_pairs={{0,4},{1,5},{2,6},{3,7},{4,0},{5,1},{6,2},{7,3},{8,12},{9,13},{10,... | collective-permute-start | bytes 1640 | tf_op jit(solution)/shard_map/ppermute | solution.py:149
  132.0 1.0 collective-permute-done.3
  133.0 1.2 concatenate.20.list_ref
  134.2 13.1 %near_pairs.1 = (f32[1024,1024]{1,0:T(8,128)}, f32[1024,128]{1,0:T(8,128)}) custom-call(s32[1]{0:T(128)} %bitcast.core_ref, s32[9,136]{1,0:T(8,128)} %concatenate.20.list_ref, bf16[1024,1024]{1,0:T(8,128)(2,1)} %normalize.1.u_ref, f32[1024,1024]{1,0:T(8,128)} %get-tuple-element.8.acc_in, f32[1024,128]{1,0:T(8,128)} %get-tuple-element.9.kacc_in, ...), custom_call_target="tpu_custom_call" | custom-call | flops 805306368 | bytes 8388608 | tf_op jit(solution)/shard_map/near_pairs/pallas_call | solution.py:183
  147.3 7.3 %opposite_pairs.1 = (bf16[1024,1024]{1,0:T(8,128)(2,1)}, f32[8,128]{1,0:T(8,128)}) custom-call(s32[1]{0:T(128)} %bitcast.core_ref, s32[9,136]{1,0:T(8,128)} %concatenate.20.list_ref, bf16[1024,1024]{1,0:T(8,128)(2,1)} %normalize.1.u_ref, f32[1024,1024]{1,0:T(8,128)} %get-tuple-element.10.acc_in, f32[1024,128]{1,0:T(8,128)} %get-tuple-element.11.kacc_in, ...), custom_call_target="tpu_custom_call" | custom-call | flops 536870912 | bytes 8388608 | tf_op jit(solution)/shard_map/opposite_pairs/pallas_call | solution.py:193
  (29 shorter events, 0.5 us)
Async XLA Ops:
  4.8 30.9 %copy-start = (bf16[1024,1024]{1,0:T(8,128)(2,1)S(1)}, bf16[1024,1024]{1,0:T(8,128)(2,1)}, u32[]{:S(2)}) copy-start(bf16[1024,1024]{1,0:T(8,128)(2,1)} %normalize.1.u_ref) | copy-start | bytes 6291460
  6.7 26.4 %collective-permute-start.8 = (bf16[512,1024]{1,0:T(8,128)(2,1)S(1)}, bf16[512,1024]{1,0:T(8,128)(2,1)S(1)}, u32[]{:S(2)}, u32[]{:S(2)}) collective-permute-start(bf16[512,1024]{1,0:T(8,128)(2,1)S(1)} %get-tuple-element.15), channel_id=1, source_target_pairs={{0,2},{1,3},{2,4},{3,5},{4,6},{5,7},{6,0},{7,1},{8,10},{9,11},{10,... | collective-permute-start | bytes 3145736 | tf_op jit(solution)/shard_map/ppermute | solution.py:19
  8.9 24.2 %collective-permute-start.6 = (bf16[512,1024]{1,0:T(8,128)(2,1)S(1)}, bf16[512,1024]{1,0:T(8,128)(2,1)S(1)}, u32[]{:S(2)}, u32[]{:S(2)}) collective-permute-start(bf16[512,1024]{1,0:T(8,128)(2,1)S(1)} %get-tuple-element.14), channel_id=1, source_target_pairs={{0,6},{1,7},{2,0},{3,1},{4,2},{5,3},{6,4},{7,5},{8,14},{9,15},{10,... | collective-permute-start | bytes 3145736 | tf_op jit(solution)/shard_map/ppermute | solution.py:19
  10.4 45.1 %collective-permute-start.9 = (bf16[512,1024]{1,0:T(8,128)(2,1)S(1)}, bf16[512,1024]{1,0:T(8,128)(2,1)S(1)}, u32[]{:S(2)}, u32[]{:S(2)}) collective-permute-start(bf16[512,1024]{1,0:T(8,128)(2,1)S(1)} %get-tuple-element.14), channel_id=1, source_target_pairs={{0,2},{1,3},{2,4},{3,5},{4,6},{5,7},{6,0},{7,1},{8,10},{9,11},{10,... | collective-permute-start | bytes 3145736 | tf_op jit(solution)/shard_map/ppermute | solution.py:19
  10.4 48.5 %collective-permute-start.5 = (bf16[512,1024]{1,0:T(8,128)(2,1)S(1)}, bf16[512,1024]{1,0:T(8,128)(2,1)S(1)}, u32[]{:S(2)}, u32[]{:S(2)}) collective-permute-start(bf16[512,1024]{1,0:T(8,128)(2,1)S(1)} %get-tuple-element.15), channel_id=1, source_target_pairs={{0,6},{1,7},{2,0},{3,1},{4,2},{5,3},{6,4},{7,5},{8,14},{9,15},{10,... | collective-permute-start | bytes 3145736 | tf_op jit(solution)/shard_map/ppermute | solution.py:19
  33.1 44.9 %collective-permute-start.11 = (bf16[512,1024]{1,0:T(8,128)(2,1)S(1)}, bf16[512,1024]{1,0:T(8,128)(2,1)S(1)}, u32[]{:S(2)}, u32[]{:S(2)}) collective-permute-start(bf16[512,1024]{1,0:T(8,128)(2,1)S(1)} %collective-permute-done.8), channel_id=1, source_target_pairs={{0,2},{1,3},{2,4},{3,5},{4,6},{5,7},{6,0},{7,1},{8,10},{9,11},{10,... | collective-permute-start | bytes 3145736 | tf_op jit(solution)/shard_map/ppermute | solution.py:19
  33.1 46.0 %collective-permute-start.12 = (bf16[512,1024]{1,0:T(8,128)(2,1)S(1)}, bf16[512,1024]{1,0:T(8,128)(2,1)S(1)}, u32[]{:S(2)}, u32[]{:S(2)}) collective-permute-start(bf16[512,1024]{1,0:T(8,128)(2,1)S(1)} %collective-permute-done.6), channel_id=1, source_target_pairs={{0,6},{1,7},{2,0},{3,1},{4,2},{5,3},{6,4},{7,5},{8,14},{9,15},{10,... | collective-permute-start | bytes 3145736 | tf_op jit(solution)/shard_map/ppermute | solution.py:19
  35.7 98.4 %collective-permute-start.4 = (bf16[1024,1024]{1,0:T(8,128)(2,1)S(1)}, bf16[1024,1024]{1,0:T(8,128)(2,1)}, u32[]{:S(2)}, u32[]{:S(2)}) collective-permute-start(bf16[1024,1024]{1,0:T(8,128)(2,1)S(1)} %copy-done), channel_id=1, source_target_pairs={{0,1},{1,0},{2,3},{3,2},{4,5},{5,4},{6,7},{7,6},{8,9},{9,8},{10,11... | collective-permute-start | bytes 6291464 | tf_op jit(solution)/shard_map/ppermute | solution.py:23
  56.6 77.6 %collective-permute-start.10 = (bf16[1024,1024]{1,0:T(8,128)(2,1)}, bf16[1024,1024]{1,0:T(8,128)(2,1)}, u32[]{:S(2)}, u32[]{:S(2)}) collective-permute-start(bf16[1024,1024]{1,0:T(8,128)(2,1)} %constant_dynamic-update-slice_fusion.2.refs_3_), channel_id=1, source_target_pairs={{0,1},{1,0},{2,3},{3,2},{4,5},{5,4},{6,7},{7,6},{8,9},{9,8},{10,11... | collective-permute-start | bytes 6291464 | tf_op jit(solution)/shard_map/ppermute | solution.py:23
  61.0 20.5 %copy-start.2 = (s32[1,1,5,64,2]{3,4,2,1,0:T(2,128)S(1)}, s32[1,1,5,64,2]{3,4,2,1,0:T(2,128)}, u32[]{:S(2)}) copy-start(s32[1,1,5,64,2]{3,4,2,1,0:T(2,128)} %param.5) | copy-start | bytes 7684
  61.0 20.9 %copy-start.4 = (s32[1,1,5]{2,1,0:T(1,128)S(1)}, s32[1,1,5]{2,1,0:T(1,128)}, u32[]{:S(2)}) copy-start(s32[1,1,5]{2,1,0:T(1,128)} %param.6) | copy-start | bytes 64
  61.0 24.4 %copy-start.3 = (s32[1,1,16,3]{2,1,3,0:T(1,128)S(1)}, s32[1,1,16,3]{2,1,3,0:T(1,128)}, u32[]{:S(2)}) copy-start(s32[1,1,16,3]{2,1,3,0:T(1,128)} %param.7) | copy-start | bytes 580
  61.0 73.2 %collective-permute-start.7 = (bf16[1024,1024]{1,0:T(8,128)(2,1)}, bf16[1024,1024]{1,0:T(8,128)(2,1)}, u32[]{:S(2)}, u32[]{:S(2)}) collective-permute-start(bf16[1024,1024]{1,0:T(8,128)(2,1)} %constant_dynamic-update-slice_fusion.refs_1_), channel_id=1, source_target_pairs={{0,1},{1,0},{2,3},{3,2},{4,5},{5,4},{6,7},{7,6},{8,9},{9,8},{10,11... | collective-permute-start | bytes 6291464 | tf_op jit(solution)/shard_map/ppermute | solution.py:23
  80.1 67.2 %collective-permute-start.13 = (bf16[1024,1024]{1,0:T(8,128)(2,1)}, bf16[1024,1024]{1,0:T(8,128)(2,1)}, u32[]{:S(2)}, u32[]{:S(2)}) collective-permute-start(bf16[1024,1024]{1,0:T(8,128)(2,1)} %constant_dynamic-update-slice_fusion.4.refs_0_.refs_1_), channel_id=1, source_target_pairs={{0,1},{1,0},{2,3},{3,2},{4,5},{5,4},{6,7},{7,6},{8,9},{9,8},{10,11... | collective-permute-start | bytes 6291464 | tf_op jit(solution)/shard_map/ppermute | solution.py:23
  82.7 2.4 %collective-permute-start = (s32[1,136]{1,0:T(1,128)S(1)}, s32[1,136]{1,0:T(1,128)S(1)}, u32[]{:S(2)}, u32[]{:S(2)}) collective-permute-start(s32[1,136]{1,0:T(1,128)S(1)} %get-tuple-element.19), channel_id=1, source_target_pairs={{0,1},{1,2},{2,3},{3,4},{4,5},{5,6},{6,7},{7,0},{8,9},{9,10},{10,1... | collective-permute-start | bytes 1640 | tf_op jit(solution)/shard_map/ppermute | solution.py:149
  85.1 3.6 %collective-permute-start.1 = (s32[1,136]{1,0:T(1,128)S(1)}, s32[1,136]{1,0:T(1,128)S(1)}, u32[]{:S(2)}, u32[]{:S(2)}) collective-permute-start(s32[1,136]{1,0:T(1,128)S(1)} %get-tuple-element.18), channel_id=1, source_target_pairs={{0,2},{1,3},{2,4},{3,5},{4,6},{5,7},{6,0},{7,1},{8,10},{9,11},{10,... | collective-permute-start | bytes 1640 | tf_op jit(solution)/shard_map/ppermute | solution.py:149
  88.8 11.6 %collective-permute-start.2 = (s32[1,136]{1,0:T(1,128)S(1)}, s32[1,136]{1,0:T(1,128)S(1)}, u32[]{:S(2)}, u32[]{:S(2)}) collective-permute-start(s32[1,136]{1,0:T(1,128)S(1)} %get-tuple-element.17), channel_id=1, source_target_pairs={{0,3},{1,4},{2,5},{3,6},{4,7},{5,0},{6,1},{7,2},{8,11},{9,12},{10,... | collective-permute-start | bytes 1640 | tf_op jit(solution)/shard_map/ppermute | solution.py:149
  90.8 42.1 %copy-start.1 = (s32[5,136]{1,0:T(8,128)S(1)}, s32[5,136]{1,0:T(8,128)}, u32[]{:S(2)}) copy-start(s32[5,136]{1,0:T(8,128)} %get-tuple-element.21.list_ref) | copy-start | bytes 8164
  100.4 32.6 %collective-permute-start.3 = (s32[1,136]{1,0:T(1,128)S(1)}, s32[1,136]{1,0:T(1,128)S(1)}, u32[]{:S(2)}, u32[]{:S(2)}) collective-permute-start(s32[1,136]{1,0:T(1,128)S(1)} %get-tuple-element.16), channel_id=1, source_target_pairs={{0,4},{1,5},{2,6},{3,7},{4,0},{5,1},{6,2},{7,3},{8,12},{9,13},{10,... | collective-permute-start | bytes 1640 | tf_op jit(solution)/shard_map/ppermute | solution.py:149
